TPU v7x, 32 devices: a whole 2x2x4 slice. The times are simulated.
32 devices in a mesh: dp: 2 (over x), ctx: 4 (over y, core), tp: 4 (over z).
Axes of the slice: x: 2, y: 2, z: 4, core: 2. Of those that a mesh axis runs over, the one named last changes fastest.
Arguments:
- query_rows: bfloat16 [2, 1536, 4096], P('dp', 'ctx', 'tp'), may hold values from -2.5 to 2.5
- key_rows: bfloat16 [2, 1536, 512], P('dp', 'ctx', 'tp'), may hold values from -2.5 to 2.5
- value_rows: bfloat16 [2, 1536, 512], P('dp', 'ctx', 'tp'), may hold values from -6 to 6
- out_grad: bfloat16 [2, 1536, 4096], P('dp', 'ctx', 'tp'), may hold values from -6 to 6
- assistant: int32 [2, 12], P('dp'), may hold values from 0 to 1, as said below
- turn_first: int32 [2, 12], P('dp'), may hold values from 0 to 11, as said below
Outputs:
- query_grad: bfloat16 [2, 1536, 4096], P('dp', 'ctx', 'tp')
- key_grad: bfloat16 [2, 1536, 512], P('dp', 'ctx', 'tp')
- value_grad: bfloat16 [2, 1536, 512], P('dp', 'ctx', 'tp')
Inputs may be any that keep to these rules, and one draw needn't show every extreme that they name: Among the 3 blocks at positions d * 3 to d * 3 + 2 at most 2 are assistant blocks, and in every sequence some such group holds exactly 2. Turns are runs of whole blocks: turn_first never falls, equals the block's own index where a turn begins, and q - 4 <= turn_first[q] <= q; in every sequence some block has q - turn_first[q] = 4.
All inputs are finite; a program needn't handle non-finite values.
Results may differ from a plain program's by a relative error of at most 0.005.
Values may be sent and summed in bfloat16 or wider, within the bound.
No kernel may reach another device: no remote copies, remote signals or barrier semaphores. Data moves between devices by JAX's collectives and lax.ppermute only.
A program may use at most 64 MiB of HBM per device.

v0:
```python
import math

import jax
import jax.numpy as jnp
from jax import lax
from jax.experimental import pallas as pl
from jax.experimental.pallas import tpu as pltpu
from jax.sharding import PartitionSpec as P

BLK = 128
SUB = 8
CHUNK = 256
F32 = jnp.float32
BF16 = jnp.bfloat16
MIB = 1 << 20


def shifted(block, axis, distance):
    devices = range(lax.axis_size(axis))
    route = [(i - distance, i) for i in devices if i - distance in devices]
    return lax.ppermute(block, axis, route)


def vmem(array):
    return pltpu.with_memory_space_constraint(array, pltpu.VMEM)


def smem(array):
    return pltpu.with_memory_space_constraint(array, pltpu.SMEM)


def hbm(array):
    return pltpu.with_memory_space_constraint(array, pltpu.HBM)


def nt_dot(left, right):
    return lax.dot_general(left, right, (((1,), (1,)), ((), ())), preferred_element_type=F32)


def nn_dot(left, right):
    return lax.dot_general(left, right, (((1,), (0,)), ((), ())), preferred_element_type=F32)


def fold(tile):
    return jnp.sum(tile.reshape(tile.shape[0] // SUB, SUB, tile.shape[1]), axis=0)


def slots_of(assistant, turn_first, base, block_count, slot_count):
    found = jnp.int32(0)
    blocks = [jnp.int32(0)] * slot_count
    starts = [jnp.int32(0)] * slot_count
    for i in range(block_count):
        mark = assistant[0, base + i]
        start = turn_first[0, base + i] - base
        for s in range(slot_count):
            here = (mark == 1) & (found == s)
            blocks[s] = jnp.where(here, i, blocks[s])
            starts[s] = jnp.where(here, start, starts[s])
        found = found + jnp.where(mark == 1, 1, 0)
    return [(blocks[s], found > s, starts[s]) for s in range(slot_count)]


def pack_kernel(key_ref, value_ref, assistant_ref, turn_ref, near_ref, far_ref, assistant, turn_first,
                sem):
    far_rows = far_ref.shape[1]
    first = near_ref.shape[1] - far_rows
    copies = [
        pltpu.make_async_copy(assistant_ref, assistant, sem.at[4]),
        pltpu.make_async_copy(turn_ref, turn_first, sem.at[5]),
    ]
    for i, source in enumerate((key_ref, value_ref)):
        copies.append(pltpu.make_async_copy(source.at[0], near_ref.at[i], sem.at[2 * i]))
        copies.append(
            pltpu.make_async_copy(
                source.at[0, pl.ds(first, far_rows)], far_ref.at[i], sem.at[2 * i + 1]
            )
        )
    for copy in copies:
        copy.start()
    for copy in copies:
        copy.wait()


def score_pass(key_tile, value_tile, query_ref, grad_ref, slot, keep, weight_ref, prob_ref, rows,
               sum_ref, dot_ref, scale):
    columns = query_ref.shape[1]
    for c in range(0, columns, CHUNK):
        span = slice(c, c + CHUNK)
        scores = nt_dot(key_tile, query_ref[slot, span, :])
        prob_grad = nt_dot(value_tile, grad_ref[slot, span, :])
        weights = jnp.exp2(scores * scale)
        if keep is not None:
            weights = jnp.where(jnp.concatenate([keep] * (CHUNK // BLK), axis=1), weights, 0.0)
        weight_ref[slot, rows, span] = weights
        prob_ref[slot, rows, span] = prob_grad
        sum_ref[slot, :, span] += fold(weights)
        dot_ref[slot, :, span] += fold(weights * prob_grad)


def grad_pass(weight_ref, prob_ref, query_ref, grad_ref, slot, rows, inverse_ref, delta_ref, low_ref,
              score_ref, score_rows, key_acc, value_acc, acc_rows):
    columns = query_ref.shape[1]
    for c in range(0, columns, CHUNK):
        span = slice(c, c + CHUNK)
        shape = (BLK // SUB, SUB, CHUNK)
        attention = weight_ref[slot, rows, span].reshape(shape) * inverse_ref[slot, :, span][None]
        lifted = prob_ref[slot, rows, span].reshape(shape) - delta_ref[slot, :, span][None]
        score_grad = (attention * lifted).reshape(BLK, CHUNK)
        low_ref[:, span] = attention.reshape(BLK, CHUNK).astype(BF16)
        score_ref[slot, score_rows, span] = score_grad.astype(BF16)
    value_acc[acc_rows, :] += nn_dot(low_ref[...], grad_ref[slot])
    key_acc[acc_rows, :] += nn_dot(score_ref[slot, score_rows, :], query_ref[slot])


def block_rows(index):
    return pl.ds(pl.multiple_of(index * BLK, BLK), BLK)


def local_kernel(sizes, assistant, turn_first, query_hbm, grad_hbm, kv_ref, query_ref, grad_ref,
                 weight_ref, prob_ref, sum_ref, dot_ref, sem):
    block_count, slot_count, head_count, width, scale = sizes
    base = lax.axis_index("ctx") * block_count
    slots = slots_of(assistant, turn_first, base, block_count, slot_count)

    def copies(s, block):
        for i, (source, target) in enumerate(((query_hbm, query_ref), (grad_hbm, grad_ref))):
            for h in range(head_count):
                yield pltpu.make_async_copy(
                    source.at[0, block_rows(block), pl.ds(h * width, width)],
                    target.at[s, pl.ds(h * BLK, BLK)],
                    sem.at[s, i, h],
                )

    for s, (block, live, start) in enumerate(slots):
        @pl.when(live)
        def _():
            for copy in copies(s, block):
                copy.start()
    sum_ref[...] = jnp.zeros_like(sum_ref)
    dot_ref[...] = jnp.zeros_like(dot_ref)
    ahead = lax.broadcasted_iota(jnp.int32, (BLK, BLK), 1) - lax.broadcasted_iota(
        jnp.int32, (BLK, BLK), 0
    )
    for s, (block, live, start) in enumerate(slots):
        @pl.when(live)
        def _():
            for copy in copies(s, block):
                copy.wait()

            def step(k, carry):
                rows = block_rows(k)
                keep = ahead >= (k - block) * BLK
                score_pass(kv_ref[0, rows, :], kv_ref[1, rows, :], query_ref, grad_ref, s, keep,
                           weight_ref, prob_ref, rows, sum_ref, dot_ref, scale * math.log2(math.e))
                return carry

            lax.fori_loop(jnp.maximum(start, 0), block + 1, step, 0)


def remote_kernel(sizes, assistant, turn_first, query_ref, grad_ref, sum_in, dot_in, near_ref, far_ref,
                  near_out, far_out, score_ref, inverse_ref, delta_ref,
                  window, weight_ref, prob_ref, sum_ref, dot_ref, low_ref, key_acc, value_acc):
    block_count, slot_count, head_count, width, scale = sizes
    base = lax.axis_index("ctx") * block_count
    slots = slots_of(assistant, turn_first, base, block_count, slot_count)
    far_rows = far_ref.shape[1]
    reach = window.shape[1] // BLK
    window[:, :far_rows, :] = far_ref[...]
    window[:, far_rows:, :] = near_ref[...]
    key_acc[...] = jnp.zeros_like(key_acc)
    value_acc[...] = jnp.zeros_like(value_acc)
    sum_ref[...] = sum_in[...]
    dot_ref[...] = dot_in[...]
    for s, (block, live, start) in enumerate(slots):
        @pl.when(live)
        def _():
            first = jnp.minimum(start + reach, reach)

            def score_step(k, carry):
                rows = block_rows(k)
                score_pass(window[0, rows, :], window[1, rows, :], query_ref, grad_ref, s, None,
                           weight_ref, prob_ref, rows, sum_ref, dot_ref, scale * math.log2(math.e))
                return carry

            lax.fori_loop(first, reach, score_step, 0)
            inverse = 1.0 / jnp.sum(sum_ref[s], axis=0, keepdims=True)
            delta = jnp.sum(dot_ref[s], axis=0, keepdims=True) * inverse
            inverse_ref[s] = jnp.broadcast_to(inverse, inverse_ref.shape[1:])
            delta_ref[s] = jnp.broadcast_to(delta, delta_ref.shape[1:])

            def grad_step(k, carry):
                rows = block_rows(k)
                grad_pass(weight_ref, prob_ref, query_ref, grad_ref, s, rows, inverse_ref, delta_ref,
                          low_ref, score_ref, rows, key_acc, value_acc, rows)
                return carry

            lax.fori_loop(first, reach, grad_step, 0)
    key_low = (key_acc[...] * scale).astype(BF16)
    value_low = value_acc[...].astype(BF16)
    far_out[0] = key_low[:far_rows]
    far_out[1] = value_low[:far_rows]
    near_out[0] = key_low[far_rows:]
    near_out[1] = value_low[far_rows:]


def finish_kernel(sizes, assistant, turn_first, query_ref, grad_ref, weight_ref, prob_ref, score_in,
                  inverse_ref, delta_ref, kv_ref, near_ref, far_ref, query_out, key_acc, value_acc,
                  score_ref, low_ref, query_acc):
    block_count, slot_count, head_count, width, scale = sizes
    base = lax.axis_index("ctx") * block_count
    slots = slots_of(assistant, turn_first, base, block_count, slot_count)
    far_blocks = far_ref.shape[1] // BLK
    reach = block_count + far_blocks
    key_acc[...] = jnp.zeros_like(key_acc)
    value_acc[...] = jnp.zeros_like(value_acc)
    query_out[...] = jnp.zeros_like(query_out)
    for s, (block, live, start) in enumerate(slots):
        @pl.when(live)
        def _():
            query_acc[...] = jnp.zeros_like(query_acc)

            def add_query(key_tile, score_source, rows):
                turned = key_tile.T
                for c in range(0, query_acc.shape[1], CHUNK):
                    span = slice(c, c + CHUNK)
                    query_acc[:, span] += nn_dot(turned, score_source[s, rows, span])

            def far_step(k, carry):
                add_query(far_ref[0, block_rows(k), :], score_in, block_rows(k))
                return carry

            def near_step(k, carry):
                add_query(near_ref[0, block_rows(k - far_blocks), :], score_in, block_rows(k))
                return carry

            def local_step(k, carry):
                rows = block_rows(k)
                grad_pass(weight_ref, prob_ref, query_ref, grad_ref, s, rows, inverse_ref, delta_ref,
                          low_ref, score_ref, rows, key_acc, value_acc, rows)
                add_query(kv_ref[0, rows, :], score_ref, rows)
                return carry

            first = jnp.minimum(start + reach, reach)
            lax.fori_loop(first, far_blocks, far_step, 0)
            lax.fori_loop(jnp.maximum(first, far_blocks), reach, near_step, 0)
            lax.fori_loop(jnp.maximum(start, 0), block + 1, local_step, 0)
            for h in range(head_count):
                turned = (query_acc[:, h * BLK:(h + 1) * BLK] * scale).T
                query_out[0, block_rows(block), h * width:(h + 1) * width] = turned.astype(BF16)
    key_acc[...] = key_acc[...] * scale


def total_kernel(key_acc, value_acc, near_ref, far_ref, key_out, value_out):
    far_rows = far_ref.shape[1]
    split = near_ref.shape[1] - far_rows
    for i, (acc, out) in enumerate(((key_acc, key_out), (value_acc, value_out))):
        total = acc[...] + near_ref[i].astype(F32)
        out[0, :split] = total[:split].astype(BF16)
        out[0, split:] = (total[split:] + far_ref[i].astype(F32)).astype(BF16)


def per_device(query_rows, key_rows, value_rows, out_grad, assistant, turn_first):
    token_count = query_rows.shape[1]
    width = key_rows.shape[2]
    head_count = query_rows.shape[2] // width
    block_count = token_count // BLK
    far_rows = block_count // 2 * BLK
    reach_rows = token_count + far_rows
    slot_count = (block_count + 1) // 2
    columns = head_count * BLK
    sizes = (block_count, slot_count, head_count, width, 1.0 / math.sqrt(width))
    any_spec = pl.BlockSpec(memory_space=pl.ANY)
    smem_spec = pl.BlockSpec(memory_space=pltpu.SMEM)
    vmem_spec = pl.BlockSpec(memory_space=pltpu.VMEM)

    def call(kernel, inputs, in_specs, outputs, out_specs, scratch, limit, macs):
        return pl.pallas_call(
            kernel,
            out_shape=outputs,
            in_specs=in_specs,
            out_specs=out_specs,
            scratch_shapes=scratch,
            compiler_params=pltpu.CompilerParams(vmem_limit_bytes=limit * MIB),
            cost_estimate=pl.CostEstimate(flops=2 * macs, bytes_accessed=2 * MIB, transcendentals=0),
        )(*inputs)

    pair = columns * BLK * width
    near, far, assistant, turn_first = call(
        pack_kernel,
        tuple(hbm(a) for a in (key_rows, value_rows, assistant, turn_first)),
        [any_spec] * 4,
        (
            pltpu.VMEM((2, token_count, width), BF16),
            pltpu.VMEM((2, far_rows, width), BF16),
            pltpu.SMEM(assistant.shape, jnp.int32),
            pltpu.SMEM(turn_first.shape, jnp.int32),
        ),
        [vmem_spec] * 2 + [smem_spec] * 2,
        [pltpu.SemaphoreType.DMA((6,))],
        8,
        BLK,
    )
    assistant, turn_first = smem(assistant), smem(turn_first)
    near_in = shifted(near, "ctx", 1)
    far_in = shifted(far, "ctx", 2)
    slot_rows = (slot_count, columns, width)
    stat_rows = (slot_count, SUB, columns)
    query_slots, grad_slots, weights, prob_grad, sums, dots = call(
        lambda *refs: local_kernel(sizes, *refs),
        (assistant, turn_first, hbm(query_rows), hbm(out_grad), vmem(near)),
        [smem_spec] * 2 + [any_spec] * 2 + [vmem_spec],
        (
            pltpu.VMEM(slot_rows, BF16),
            pltpu.VMEM(slot_rows, BF16),
            pltpu.VMEM((slot_count, token_count, columns), F32),
            pltpu.VMEM((slot_count, token_count, columns), F32),
            pltpu.VMEM(stat_rows, F32),
            pltpu.VMEM(stat_rows, F32),
        ),
        [vmem_spec] * 6,
        [pltpu.SemaphoreType.DMA((slot_count, 2, head_count))],
        16,
        10 * pair,
    )
    near_grad, far_grad, score_grad, inverse, delta = call(
        lambda *refs: remote_kernel(sizes, *refs),
        (assistant, turn_first)
        + tuple(vmem(a) for a in (query_slots, grad_slots, sums, dots, near_in, far_in)),
        [smem_spec] * 2 + [vmem_spec] * 6,
        (
            pltpu.VMEM((2, token_count, width), BF16),
            pltpu.VMEM((2, far_rows, width), BF16),
            pltpu.VMEM((slot_count, reach_rows, columns), BF16),
            pltpu.VMEM(stat_rows, F32),
            pltpu.VMEM(stat_rows, F32),
        ),
        [vmem_spec] * 5,
        [
            pltpu.VMEM((2, reach_rows, width), BF16),
            pltpu.VMEM((slot_count, reach_rows, columns), F32),
            pltpu.VMEM((slot_count, reach_rows, columns), F32),
            pltpu.VMEM(stat_rows, F32),
            pltpu.VMEM(stat_rows, F32),
            pltpu.VMEM((BLK, columns), BF16),
            pltpu.VMEM((reach_rows, width), F32),
            pltpu.VMEM((reach_rows, width), F32),
        ],
        20,
        20 * pair,
    )
    near_back = shifted(near_grad, "ctx", -1)
    far_back = shifted(far_grad, "ctx", -2)
    query_grad, key_acc, value_acc = call(
        lambda *refs: finish_kernel(sizes, *refs),
        (assistant, turn_first)
        + tuple(
            vmem(a)
            for a in (query_slots, grad_slots, weights, prob_grad, score_grad, inverse, delta, near,
                      near_in, far_in)
        ),
        [smem_spec] * 2 + [vmem_spec] * 10,
        (
            jax.ShapeDtypeStruct(query_rows.shape, BF16),
            pltpu.VMEM((token_count, width), F32),
            pltpu.VMEM((token_count, width), F32),
        ),
        [vmem_spec] * 3,
        [
            pltpu.VMEM((slot_count, token_count, columns), BF16),
            pltpu.VMEM((BLK, columns), BF16),
            pltpu.VMEM((BLK, columns), F32),
        ],
        16,
        25 * pair,
    )
    key_grad, value_grad = call(
        total_kernel,
        tuple(vmem(a) for a in (key_acc, value_acc, near_back, far_back)),
        [vmem_spec] * 4,
        (
            jax.ShapeDtypeStruct(key_rows.shape, BF16),
            jax.ShapeDtypeStruct(value_rows.shape, BF16),
        ),
        [vmem_spec] * 2,
        [],
        8,
        BLK,
    )
    return (query_grad, key_grad, value_grad)


def solution(mesh):
    return jax.shard_map(
        per_device,
        mesh=mesh,
        in_specs=(
            P("dp", "ctx", "tp"),
            P("dp", "ctx", "tp"),
            P("dp", "ctx", "tp"),
            P("dp", "ctx", "tp"),
            P("dp", None),
            P("dp", None),
        ),
        out_specs=(P("dp", "ctx", "tp"), P("dp", "ctx", "tp"), P("dp", "ctx", "tp")),
        check_vma=False,
    )
```

profile of v0, /device:TPU:2, one launch (start us, length us, event | category | flops | bytes accessed | tf_op | source)
XLA Modules:
  0.0 21.9 jit_solution(7595376672369971891)
XLA Ops:
  0.6 1.0 %shard_map.85 = (bf16[2,384,128]{2,1,0:T(8,128)(2,1)S(1)}, bf16[2,128,128]{2,1,0:T(8,128)(2,1)S(1)}, s32[1,12]{1,0:T(1,128)S(4)}, s32[1,12]{1,0:T(1,128)S(4)}) custom-call(bf16[1,384,128]{2,1,0:T(8,128)(2,1)} %key_ref.1, bf16[1,384,128]{2,1,0:T(8,128)(2,1)} %value_ref.1, s32[1,12]{1,0:T(1,128)} %assistant_ref.1, s32[1,12]{1,0:T(1,128)} %turn_ref.1), custom_call_target="tpu_custom_call" | custom-call | flops 256 | bytes 2097152 | tf_op jit(solution)/shard_map/pallas_call | solution.py:277
  1.7 1.8 %collective-permute-start = (bf16[2,384,128]{2,1,0:T(8,128)(2,1)S(1)}, bf16[2,384,128]{2,1,0:T(8,128)(2,1)S(1)}, u32[]{:S(2)}, u32[]{:S(2)}) collective-permute-start(bf16[2,384,128]{2,1,0:T(8,128)(2,1)S(1)} %get-tuple-element.25.refs_4_.refs_9_), channel_id=1, source_target_pairs={{0,4},{4,8},{8,12},{1,5},{5,9},{9,13},{2,6},{6,10},{10,14},{3,7},{... | collective-permute-start | bytes 589832 | tf_op jit(solution)/shard_map/ppermute | solution.py:21
  3.4 3.6 %collective-permute-start.1 = (bf16[2,128,128]{2,1,0:T(8,128)(2,1)S(1)}, bf16[2,128,128]{2,1,0:T(8,128)(2,1)S(1)}, u32[]{:S(2)}, u32[]{:S(2)}) collective-permute-start(bf16[2,128,128]{2,1,0:T(8,128)(2,1)S(1)} %get-tuple-element.32), channel_id=1, source_target_pairs={{0,8},{4,12},{1,9},{5,13},{2,10},{6,14},{3,11},{7,15},{16,24},{20,... | collective-permute-start | bytes 196616 | tf_op jit(solution)/shard_map/ppermute | solution.py:21
  7.0 2.3 %shard_map.86 = (bf16[2,1024,128]{2,1,0:T(8,128)(2,1)S(1)}, bf16[2,1024,128]{2,1,0:T(8,128)(2,1)S(1)}, f32[2,384,1024]{2,1,0:T(8,128)S(1)}, f32[2,384,1024]{2,1,...) custom-call(s32[1,12]{1,0:T(1,128)S(4)} %get-tuple-element.23.refs_0_, ...), custom_call_target="tpu_custom_call" | custom-call | flops 335544320 | bytes 2097152 | tf_op jit(solution)/shard_map/pallas_call | solution.py:277
  9.3 0.0 collective-permute-done.1.refs_7_.refs_11_
  9.3 0.0 collective-permute-done.refs_6_.refs_10_
  9.3 0.1 shard_map.87
  9.4 1.3 %collective-permute-start.2 = (bf16[2,384,128]{2,1,0:T(8,128)(2,1)S(1)}, bf16[2,384,128]{2,1,0:T(8,128)(2,1)S(1)}, u32[]{:S(2)}, u32[]{:S(2)}) collective-permute-start(bf16[2,384,128]{2,1,0:T(8,128)(2,1)S(1)} %get-tuple-element.39), channel_id=1, source_target_pairs={{4,0},{8,4},{12,8},{5,1},{9,5},{13,9},{6,2},{10,6},{14,10},{7,3},{... | collective-permute-start | bytes 589832 | tf_op jit(solution)/shard_map/ppermute | solution.py:21
  10.7 1.3 %collective-permute-start.3 = (bf16[2,128,128]{2,1,0:T(8,128)(2,1)S(1)}, bf16[2,128,128]{2,1,0:T(8,128)(2,1)S(1)}, u32[]{:S(2)}, u32[]{:S(2)}) collective-permute-start(bf16[2,128,128]{2,1,0:T(8,128)(2,1)S(1)} %get-tuple-element.40), channel_id=1, source_target_pairs={{8,0},{12,4},{9,1},{13,5},{10,2},{14,6},{11,3},{15,7},{24,16},{28,... | collective-permute-start | bytes 196616 | tf_op jit(solution)/shard_map/ppermute | solution.py:21
  12.0 2.3 %shard_map.88 = (bf16[1,384,1024]{2,1,0:T(8,128)(2,1)}, f32[384,128]{1,0:T(8,128)S(1)}, f32[384,128]{1,0:T(8,128)S(1)}) custom-call(s32[1,12]{1,0:T(1,128)S(4)} %get-tuple-element.23.refs_0_, s32[1,12]{1,0:T(1,128)S(4)} %get-tuple-element.24.refs_1_, bf16[2,1024,128]{2,1,0:T(8,128)(2,1)S(1)} %get-tuple-element.26.refs_2_, ...), custom_call_target="tpu_custom_call" | custom-call | flops 838860800 | bytes 2097152 | tf_op jit(solution)/shard_map/pallas_call | solution.py:277
  14.3 6.9 %collective-permute-done.3.far_ref = bf16[2,128,128]{2,1,0:T(8,128)(2,1)S(1)} collective-permute-done((bf16[2,128,128]{2,1,0:T(8,128)(2,1)S(1)}, bf16[2,128,128]{2,1,0:T(8,128)(2,1)S(1)}, u32[]{:S(2)}, u32[]{:S(2)}) %collective-permute-start.3) | collective-permute-done | bytes 65568 | tf_op jit(solution)/shard_map/ppermute | solution.py:21
  21.2 0.0 collective-permute-done.2.near_ref
  21.2 0.7 %shard_map.89 = (bf16[1,384,128]{2,1,0:T(8,128)(2,1)}, bf16[1,384,128]{2,1,0:T(8,128)(2,1)}) custom-call(f32[384,128]{1,0:T(8,128)S(1)} %get-tuple-element.37.key_acc, f32[384,128]{1,0:T(8,128)S(1)} %get-tuple-element.38.value_acc, bf16[2,384,128]{2,1,0:T(8,128)(2,1)S(1)} %collective-permute-done.2.near_ref, ...), custom_call_target="tpu_custom_call" | custom-call | flops 256 | bytes 2097152 | tf_op jit(solution)/shard_map/pallas_call | solution.py:277
Async XLA Ops:
  1.7 7.6 %collective-permute-start = (bf16[2,384,128]{2,1,0:T(8,128)(2,1)S(1)}, bf16[2,384,128]{2,1,0:T(8,128)(2,1)S(1)}, u32[]{:S(2)}, u32[]{:S(2)}) collective-permute-start(bf16[2,384,128]{2,1,0:T(8,128)(2,1)S(1)} %get-tuple-element.25.refs_4_.refs_9_), channel_id=1, source_target_pairs={{0,4},{4,8},{8,12},{1,5},{5,9},{9,13},{2,6},{6,10},{10,14},{3,7},{... | collective-permute-start | bytes 589832 | tf_op jit(solution)/shard_map/ppermute | solution.py:21
  3.4 5.9 %collective-permute-start.1 = (bf16[2,128,128]{2,1,0:T(8,128)(2,1)S(1)}, bf16[2,128,128]{2,1,0:T(8,128)(2,1)S(1)}, u32[]{:S(2)}, u32[]{:S(2)}) collective-permute-start(bf16[2,128,128]{2,1,0:T(8,128)(2,1)S(1)} %get-tuple-element.32), channel_id=1, source_target_pairs={{0,8},{4,12},{1,9},{5,13},{2,10},{6,14},{3,11},{7,15},{16,24},{20,... | collective-permute-start | bytes 196616 | tf_op jit(solution)/shard_map/ppermute | solution.py:21
  9.4 11.7 %collective-permute-start.2 = (bf16[2,384,128]{2,1,0:T(8,128)(2,1)S(1)}, bf16[2,384,128]{2,1,0:T(8,128)(2,1)S(1)}, u32[]{:S(2)}, u32[]{:S(2)}) collective-permute-start(bf16[2,384,128]{2,1,0:T(8,128)(2,1)S(1)} %get-tuple-element.39), channel_id=1, source_target_pairs={{4,0},{8,4},{12,8},{5,1},{9,5},{13,9},{6,2},{10,6},{14,10},{7,3},{... | collective-permute-start | bytes 589832 | tf_op jit(solution)/shard_map/ppermute | solution.py:21
  10.7 10.4 %collective-permute-start.3 = (bf16[2,128,128]{2,1,0:T(8,128)(2,1)S(1)}, bf16[2,128,128]{2,1,0:T(8,128)(2,1)S(1)}, u32[]{:S(2)}, u32[]{:S(2)}) collective-permute-start(bf16[2,128,128]{2,1,0:T(8,128)(2,1)S(1)} %get-tuple-element.40), channel_id=1, source_target_pairs={{8,0},{12,4},{9,1},{13,5},{10,2},{14,6},{11,3},{15,7},{24,16},{28,... | collective-permute-start | bytes 196616 | tf_op jit(solution)/shard_map/ppermute | solution.py:21
where the time goes:
time: 21.7 us; the launch traced here: 21.9 us
  starting transfers between devices  7.93 us (37%)
  waiting for transfers between devices  6.86 us (32%)
  Pallas kernels  6.36 us (29%)
  between operations  0.7 us (3%)
    ppermute x4, starting transfers between devices, shifted(): return lax.ppermute(block, axis, route)  7.93 us
    ppermute x4, waiting for transfers between devices, shifted(): return lax.ppermute(block, axis, route)  6.86 us
    pallas_call x5, Pallas kernels, call(): pl.pallas_call(kernel, out_shape=outputs, in_specs=in_specs, out_specs=ou...  6.36 us
  transfers between devices with their start and end apart: 4, of which 1 were waited for; matrix products, arithmetic and copies ran while one was open for 0% of the time, Pallas kernels for 21%

commit v1 on v0

v1 whole, which is shorter than its diff:
```python
import math

import jax
import jax.numpy as jnp
from jax import lax
from jax.experimental import pallas as pl
from jax.experimental.pallas import tpu as pltpu
from jax.sharding import PartitionSpec as P

BLK = 128
SUB = 8
CHUNK = 256
F32 = jnp.float32
BF16 = jnp.bfloat16
MIB = 1 << 20


def shifted(block, axis, distance):
    devices = range(lax.axis_size(axis))
    route = [(i - distance, i) for i in devices if i - distance in devices]
    return lax.ppermute(block, axis, route)


def vmem(array):
    return pltpu.with_memory_space_constraint(array, pltpu.VMEM)


def smem(array):
    return pltpu.with_memory_space_constraint(array, pltpu.SMEM)


def hbm(array):
    return pltpu.with_memory_space_constraint(array, pltpu.HBM)


def nt_dot(left, right):
    return lax.dot_general(left, right, (((1,), (1,)), ((), ())), preferred_element_type=F32)


def nn_dot(left, right):
    return lax.dot_general(left, right, (((1,), (0,)), ((), ())), preferred_element_type=F32)


def fold(tile):
    return jnp.sum(tile.reshape(tile.shape[0] // SUB, SUB, tile.shape[1]), axis=0)


def slots_of(assistant, turn_first, base, block_count, slot_count):
    found = jnp.int32(0)
    blocks = [jnp.int32(0)] * slot_count
    starts = [jnp.int32(0)] * slot_count
    for i in range(block_count):
        mark = assistant[0, base + i]
        start = turn_first[0, base + i] - base
        for s in range(slot_count):
            here = (mark == 1) & (found == s)
            blocks[s] = jnp.where(here, i, blocks[s])
            starts[s] = jnp.where(here, start, starts[s])
        found = found + jnp.where(mark == 1, 1, 0)
    return [(blocks[s], found > s, starts[s]) for s in range(slot_count)]


def pack_kernel(key_ref, value_ref, assistant_ref, turn_ref, near_ref, far_ref, assistant, turn_first,
                sem):
    far_rows = far_ref.shape[1]
    first = near_ref.shape[1] - far_rows
    copies = [
        pltpu.make_async_copy(assistant_ref, assistant, sem.at[4]),
        pltpu.make_async_copy(turn_ref, turn_first, sem.at[5]),
    ]
    for i, source in enumerate((key_ref, value_ref)):
        copies.append(pltpu.make_async_copy(source.at[0], near_ref.at[i], sem.at[2 * i]))
        copies.append(
            pltpu.make_async_copy(
                source.at[0, pl.ds(first, far_rows)], far_ref.at[i], sem.at[2 * i + 1]
            )
        )
    for copy in copies:
        copy.start()
    for copy in copies:
        copy.wait()


def score_pass(key_tile, value_tile, query_ref, grad_ref, slot, keep, weight_ref, prob_ref, at, sum_ref,
               dot_ref, scale):
    columns = query_ref.shape[1]
    height = key_tile.shape[0]
    for c in range(0, columns, CHUNK):
        span = slice(c, c + CHUNK)
        scores = nt_dot(key_tile, query_ref[slot, span, :])
        prob_grad = nt_dot(value_tile, grad_ref[slot, span, :])
        weights = jnp.exp2(scores * scale)
        if keep is not None:
            wide = jnp.concatenate([keep] * (CHUNK // BLK), axis=1)
            last = jnp.where(wide, weights[height - BLK:], 0.0)
            weights = jnp.concatenate([weights[:height - BLK], last], axis=0) if height > BLK else last
        weight_ref[at + (span,)] = weights
        prob_ref[at + (span,)] = prob_grad
        sum_ref[slot, :, span] = fold(weights)
        dot_ref[slot, :, span] = fold(weights * prob_grad)


def grad_pass(weight_ref, prob_ref, at, query_ref, grad_ref, slot, inverse_ref, delta_ref, low_ref,
              score_ref, score_rows, key_acc, value_acc, acc_rows):
    columns = query_ref.shape[1]
    height = acc_rows.size
    for c in range(0, columns, CHUNK):
        span = slice(c, c + CHUNK)
        shape = (height // SUB, SUB, CHUNK)
        attention = weight_ref[at + (span,)].reshape(shape) * inverse_ref[slot, :, span][None]
        lifted = prob_ref[at + (span,)].reshape(shape) - delta_ref[slot, :, span][None]
        score_grad = (attention * lifted).reshape(height, CHUNK)
        low_ref[:height, span] = attention.reshape(height, CHUNK).astype(BF16)
        score_ref[slot, score_rows, span] = score_grad.astype(BF16)
    value_acc[acc_rows, :] += nn_dot(low_ref[:height], grad_ref[slot])
    key_acc[acc_rows, :] += nn_dot(score_ref[slot, score_rows, :], query_ref[slot])


def block_rows(index, count=1):
    return pl.ds(pl.multiple_of(index * BLK, BLK), count * BLK)


def pick(values, s):
    chosen = values[0]
    for i in range(1, len(values)):
        chosen = jnp.where(s == i, values[i], chosen)
    return chosen


def over_slots(slots, body):
    def step(s, carry):
        block, start = (pick([slot[i] for slot in slots], s) for i in (0, 2))

        @pl.when(pick([jnp.where(slot[1], 1, 0) for slot in slots], s) == 1)
        def _():
            body(s, block, start)

        return carry

    lax.fori_loop(0, len(slots), step, 0)


def local_kernel(sizes, early, assistant, turn_first, query_hbm, grad_hbm, kv_ref, *rest):
    query_ref, grad_ref, weight_ref, prob_ref, sum_ref, dot_ref, sem = rest[-7:]
    block_count, slot_count, head_count, width, scale = sizes
    rank = lax.axis_index("ctx")
    first_half = rank * 2 < lax.axis_size("ctx")

    def run():
        slots = slots_of(assistant, turn_first, rank * block_count, block_count, slot_count)

        def copies(s, block):
            for i, (source, target) in enumerate(((query_hbm, query_ref), (grad_hbm, grad_ref))):
                for h in range(head_count):
                    yield pltpu.make_async_copy(
                        source.at[0, block_rows(block), pl.ds(h * width, width)],
                        target.at[s, pl.ds(h * BLK, BLK)],
                        sem.at[s, i, h],
                    )

        for s, (block, live, start) in enumerate(slots):
            @pl.when(live)
            def _():
                for copy in copies(s, block):
                    copy.start()
        keep = lax.broadcasted_iota(jnp.int32, (BLK, BLK), 0) <= lax.broadcasted_iota(
            jnp.int32, (BLK, BLK), 1
        )

        def body(s, block, start):
            for copy in copies(s, block):
                copy.wait()
            low = jnp.maximum(start, 0)
            for count in range(1, block_count + 1):
                @pl.when(block + 1 - low == count)
                def _():
                    rows = block_rows(low, count)
                    score_pass(kv_ref[0, rows, :], kv_ref[1, rows, :], query_ref, grad_ref, s, keep,
                               weight_ref, prob_ref, (s, rows), sum_ref, dot_ref,
                               scale * math.log2(math.e))

        over_slots(slots, body)

    pl.when(first_half if early else jnp.logical_not(first_half))(run)


def near_kernel(sizes, assistant, turn_first, query_ref, grad_ref, near_ref, weight_ref, prob_ref, sum_ref,
                dot_ref):
    block_count, slot_count, head_count, width, scale = sizes
    base = lax.axis_index("ctx") * block_count
    slots = slots_of(assistant, turn_first, base, block_count, slot_count)
    sum_ref[...] = jnp.zeros_like(sum_ref)
    dot_ref[...] = jnp.zeros_like(dot_ref)

    def body(s, block, start):
        for count in range(1, block_count + 1):
            last = start <= -count if count == block_count else start == -count

            @pl.when(last)
            def _():
                rows = pl.ds((block_count - count) * BLK, count * BLK)
                score_pass(near_ref[0, rows, :], near_ref[1, rows, :], query_ref, grad_ref, s, None,
                           weight_ref, prob_ref, (s, rows), sum_ref, dot_ref, scale * math.log2(math.e))

    over_slots(slots, body)


def remote_kernel(sizes, assistant, turn_first, query_ref, grad_ref, sum_local, dot_local, sum_near,
                  dot_near, weight_near, prob_near, far_ref, near_out, far_out, score_ref, inverse_ref,
                  delta_ref, weight_far, prob_far, sum_far, dot_far, low_ref, key_acc, value_acc):
    block_count, slot_count, head_count, width, scale = sizes
    base = lax.axis_index("ctx") * block_count
    slots = slots_of(assistant, turn_first, base, block_count, slot_count)
    far_rows = far_ref.shape[1]
    far_blocks = far_rows // BLK
    key_acc[...] = jnp.zeros_like(key_acc)
    value_acc[...] = jnp.zeros_like(value_acc)
    sum_far[...] = jnp.zeros_like(sum_far)
    dot_far[...] = jnp.zeros_like(dot_far)

    def body(s, block, start):
        for count in range(1, far_blocks + 1):
            @pl.when(start == -block_count - count)
            def _():
                rows = pl.ds((far_blocks - count) * BLK, count * BLK)
                score_pass(far_ref[0, rows, :], far_ref[1, rows, :], query_ref, grad_ref, s, None,
                           weight_far, prob_far, (s, rows), sum_far, dot_far, scale * math.log2(math.e))

        sums = sum_local[s] + sum_near[s] + sum_far[s]
        dots = dot_local[s] + dot_near[s] + dot_far[s]
        inverse = 1.0 / jnp.sum(sums, axis=0, keepdims=True)
        delta = jnp.sum(dots, axis=0, keepdims=True) * inverse
        inverse_ref[s] = jnp.broadcast_to(inverse, inverse_ref.shape[1:])
        delta_ref[s] = jnp.broadcast_to(delta, delta_ref.shape[1:])
        for count in range(1, far_blocks + 1):
            @pl.when(start == -block_count - count)
            def _():
                rows = pl.ds((far_blocks - count) * BLK, count * BLK)
                grad_pass(weight_far, prob_far, (s, rows), query_ref, grad_ref, s, inverse_ref, delta_ref,
                          low_ref, score_ref, rows, key_acc, value_acc, rows)

        for count in range(1, block_count + 1):
            last = start <= -count if count == block_count else start == -count

            @pl.when(last)
            def _():
                rows = pl.ds((block_count - count) * BLK, count * BLK)
                window = pl.ds(far_rows + (block_count - count) * BLK, count * BLK)
                grad_pass(weight_near, prob_near, (s, rows), query_ref, grad_ref, s, inverse_ref,
                          delta_ref, low_ref, score_ref, window, key_acc, value_acc, window)

    over_slots(slots, body)
    key_low = (key_acc[...] * scale).astype(BF16)
    value_low = value_acc[...].astype(BF16)
    far_out[0] = key_low[:far_rows]
    far_out[1] = value_low[:far_rows]
    near_out[0] = key_low[far_rows:]
    near_out[1] = value_low[far_rows:]


def finish_kernel(sizes, assistant, turn_first, query_ref, grad_ref, weight_ref, prob_ref, score_in,
                  inverse_ref, delta_ref, kv_ref, near_ref, far_ref, query_out, key_acc, value_acc,
                  score_ref, low_ref, query_acc):
    block_count, slot_count, head_count, width, scale = sizes
    base = lax.axis_index("ctx") * block_count
    slots = slots_of(assistant, turn_first, base, block_count, slot_count)
    far_blocks = far_ref.shape[1] // BLK
    reach = block_count + far_blocks
    key_acc[...] = jnp.zeros_like(key_acc)
    value_acc[...] = jnp.zeros_like(value_acc)
    query_out[...] = jnp.zeros_like(query_out)

    def body(s, block, start):
        query_acc[...] = jnp.zeros_like(query_acc)

        def add_query(key_tile, score_source, rows):
            turned = key_tile.T
            for c in range(0, query_acc.shape[1], CHUNK):
                span = slice(c, c + CHUNK)
                query_acc[:, span] += nn_dot(turned, score_source[s, rows, span])

        def far_step(k, carry):
            add_query(far_ref[0, block_rows(k), :], score_in, block_rows(k))
            return carry

        def near_step(k, carry):
            add_query(near_ref[0, block_rows(k - far_blocks), :], score_in, block_rows(k))
            return carry

        first = jnp.minimum(start + reach, reach)
        lax.fori_loop(first, far_blocks, far_step, 0)
        lax.fori_loop(jnp.maximum(first, far_blocks), reach, near_step, 0)
        low = jnp.maximum(start, 0)
        for count in range(1, block_count + 1):
            @pl.when(block + 1 - low == count)
            def _():
                rows = block_rows(low, count)
                grad_pass(weight_ref, prob_ref, (s, rows), query_ref, grad_ref, s, inverse_ref, delta_ref,
                          low_ref, score_ref, rows, key_acc, value_acc, rows)
                add_query(kv_ref[0, rows, :], score_ref, rows)

        for h in range(head_count):
            turned = (query_acc[:, h * BLK:(h + 1) * BLK] * scale).T
            query_out[0, block_rows(block), h * width:(h + 1) * width] = turned.astype(BF16)

    over_slots(slots, body)
    key_acc[...] = key_acc[...] * scale


def total_kernel(key_acc, value_acc, near_ref, far_ref, key_out, value_out):
    far_rows = far_ref.shape[1]
    split = near_ref.shape[1] - far_rows
    for i, (acc, out) in enumerate(((key_acc, key_out), (value_acc, value_out))):
        total = acc[...] + near_ref[i].astype(F32)
        out[0, :split] = total[:split].astype(BF16)
        out[0, split:] = (total[split:] + far_ref[i].astype(F32)).astype(BF16)


def per_device(query_rows, key_rows, value_rows, out_grad, assistant, turn_first):
    token_count = query_rows.shape[1]
    width = key_rows.shape[2]
    head_count = query_rows.shape[2] // width
    block_count = token_count // BLK
    far_rows = block_count // 2 * BLK
    reach_rows = token_count + far_rows
    slot_count = (block_count + 1) // 2
    columns = head_count * BLK
    sizes = (block_count, slot_count, head_count, width, 1.0 / math.sqrt(width))
    any_spec = pl.BlockSpec(memory_space=pl.ANY)
    smem_spec = pl.BlockSpec(memory_space=pltpu.SMEM)
    vmem_spec = pl.BlockSpec(memory_space=pltpu.VMEM)

    def call(kernel, inputs, in_specs, outputs, out_specs, scratch, limit, macs, aliases={}):
        return pl.pallas_call(
            kernel,
            out_shape=outputs,
            in_specs=in_specs,
            out_specs=out_specs,
            scratch_shapes=scratch,
            input_output_aliases=aliases,
            compiler_params=pltpu.CompilerParams(vmem_limit_bytes=limit * MIB),
            cost_estimate=pl.CostEstimate(flops=2 * macs, bytes_accessed=2 * MIB, transcendentals=0),
        )(*inputs)

    pair = columns * BLK * width
    near, far, assistant, turn_first = call(
        pack_kernel,
        tuple(hbm(a) for a in (key_rows, value_rows, assistant, turn_first)),
        [any_spec] * 4,
        (
            pltpu.VMEM((2, token_count, width), BF16),
            pltpu.VMEM((2, far_rows, width), BF16),
            pltpu.SMEM(assistant.shape, jnp.int32),
            pltpu.SMEM(turn_first.shape, jnp.int32),
        ),
        [vmem_spec] * 2 + [smem_spec] * 2,
        [pltpu.SemaphoreType.DMA((6,))],
        8,
        BLK,
    )
    assistant, turn_first = smem(assistant), smem(turn_first)
    slot_rows = (slot_count, columns, width)
    stat_rows = (slot_count, SUB, columns)
    local_rows = (slot_count, token_count, columns)
    local_shapes = (
        pltpu.VMEM(slot_rows, BF16),
        pltpu.VMEM(slot_rows, BF16),
        pltpu.VMEM(local_rows, F32),
        pltpu.VMEM(local_rows, F32),
        pltpu.VMEM(stat_rows, F32),
        pltpu.VMEM(stat_rows, F32),
    )
    local_inputs = (assistant, turn_first, hbm(query_rows), hbm(out_grad), vmem(near))
    local_specs = [smem_spec] * 2 + [any_spec] * 2 + [vmem_spec]
    local_sems = [pltpu.SemaphoreType.DMA((slot_count, 2, head_count))]
    local_state = call(
        lambda *refs: local_kernel(sizes, True, *refs),
        local_inputs,
        local_specs,
        local_shapes,
        [vmem_spec] * 6,
        local_sems,
        16,
        10 * pair,
    )
    near, far, local_state = lax.optimization_barrier((near, far, local_state))
    near_in = shifted(near, "ctx", 1)
    far_in = shifted(far, "ctx", 2)
    local_state = call(
        lambda *refs: local_kernel(sizes, False, *refs),
        local_inputs + tuple(vmem(a) for a in local_state),
        local_specs + [vmem_spec] * 6,
        local_shapes,
        [vmem_spec] * 6,
        local_sems,
        16,
        10 * pair,
        {5 + i: i for i in range(6)},
    )
    query_slots, grad_slots, weights, prob_grad, sums, dots = local_state
    weight_near, prob_near, sum_near, dot_near = call(
        lambda *refs: near_kernel(sizes, *refs),
        (assistant, turn_first) + tuple(vmem(a) for a in (query_slots, grad_slots, near_in)),
        [smem_spec] * 2 + [vmem_spec] * 3,
        local_shapes[2:],
        [vmem_spec] * 4,
        [],
        16,
        10 * pair,
    )
    near_grad, far_grad, score_grad, inverse, delta = call(
        lambda *refs: remote_kernel(sizes, *refs),
        (assistant, turn_first)
        + tuple(
            vmem(a)
            for a in (query_slots, grad_slots, sums, dots, sum_near, dot_near, weight_near, prob_near,
                      far_in)
        ),
        [smem_spec] * 2 + [vmem_spec] * 9,
        (
            pltpu.VMEM((2, token_count, width), BF16),
            pltpu.VMEM((2, far_rows, width), BF16),
            pltpu.VMEM((slot_count, reach_rows, columns), BF16),
            pltpu.VMEM(stat_rows, F32),
            pltpu.VMEM(stat_rows, F32),
        ),
        [vmem_spec] * 5,
        [
            pltpu.VMEM((slot_count, far_rows, columns), F32),
            pltpu.VMEM((slot_count, far_rows, columns), F32),
            pltpu.VMEM(stat_rows, F32),
            pltpu.VMEM(stat_rows, F32),
            pltpu.VMEM((token_count, columns), BF16),
            pltpu.VMEM((reach_rows, width), F32),
            pltpu.VMEM((reach_rows, width), F32),
        ],
        20,
        14 * pair,
    )
    near_back = shifted(near_grad, "ctx", -1)
    far_back = shifted(far_grad, "ctx", -2)
    query_grad, key_acc, value_acc = call(
        lambda *refs: finish_kernel(sizes, *refs),
        (assistant, turn_first)
        + tuple(
            vmem(a)
            for a in (query_slots, grad_slots, weights, prob_grad, score_grad, inverse, delta, near,
                      near_in, far_in)
        ),
        [smem_spec] * 2 + [vmem_spec] * 10,
        (
            jax.ShapeDtypeStruct(query_rows.shape, BF16),
            pltpu.VMEM((token_count, width), F32),
            pltpu.VMEM((token_count, width), F32),
        ),
        [vmem_spec] * 3,
        [
            pltpu.VMEM((slot_count, token_count, columns), BF16),
            pltpu.VMEM((token_count, columns), BF16),
            pltpu.VMEM((BLK, columns), F32),
        ],
        16,
        25 * pair,
    )
    key_grad, value_grad = call(
        total_kernel,
        tuple(vmem(a) for a in (key_acc, value_acc, near_back, far_back)),
        [vmem_spec] * 4,
        (
            jax.ShapeDtypeStruct(key_rows.shape, BF16),
            jax.ShapeDtypeStruct(value_rows.shape, BF16),
        ),
        [vmem_spec] * 2,
        [],
        8,
        BLK,
    )
    return (query_grad, key_grad, value_grad)


def solution(mesh):
    return jax.shard_map(
        per_device,
        mesh=mesh,
        in_specs=(
            P("dp", "ctx", "tp"),
            P("dp", "ctx", "tp"),
            P("dp", "ctx", "tp"),
            P("dp", "ctx", "tp"),
            P("dp", None),
            P("dp", None),
        ),
        out_specs=(P("dp", "ctx", "tp"), P("dp", "ctx", "tp"), P("dp", "ctx", "tp")),
        check_vma=False,
    )
```

time: 21.7 us -> 21.4 us (0.986)
  the two profiles are of different devices: /device:TPU:2 before, /device:TPU:0 now
where the time goes in v1:
time: 21.4 us; the launch traced here: 21.1 us
  starting transfers between devices  7.42 us (35%)
  Pallas kernels  7.06 us (33%)
  waiting for transfers between devices  5.9 us (28%)
  between operations  0.71 us (3%)
    ppermute x4, starting transfers between devices, shifted(): return lax.ppermute(block, axis, route)  7.42 us
    pallas_call x7, Pallas kernels, call(): pl.pallas_call(kernel, out_shape=outputs, in_specs=in_specs, out_specs=ou...  7.06 us
    ppermute x4, waiting for transfers between devices, shifted(): return lax.ppermute(block, axis, route)  5.9 us
  transfers between devices with their start and end apart: 4, of which 2 were waited for; matrix products, arithmetic and copies ran while one was open for 0% of the time, Pallas kernels for 14%

profile of v1, /device:TPU:0, one launch (start us, length us, event | category | flops | bytes accessed | tf_op | source)
XLA Modules:
  0.0 21.1 jit_solution(3284782575016106579)
XLA Ops:
  0.6 1.0 %shard_map.85 = (bf16[2,384,128]{2,1,0:T(8,128)(2,1)S(1)}, bf16[2,128,128]{2,1,0:T(8,128)(2,1)S(1)}, s32[1,12]{1,0:T(1,128)S(4)}, s32[1,12]{1,0:T(1,128)S(4)}) custom-call(bf16[1,384,128]{2,1,0:T(8,128)(2,1)} %key_ref.1, bf16[1,384,128]{2,1,0:T(8,128)(2,1)} %value_ref.1, s32[1,12]{1,0:T(1,128)} %assistant_ref.1, s32[1,12]{1,0:T(1,128)} %turn_ref.1), custom_call_target="tpu_custom_call" | custom-call | flops 256 | bytes 2097152 | tf_op jit(solution)/shard_map/pallas_call | solution.py:334
  1.7 2.3 %shard_map.86 = (bf16[2,1024,128]{2,1,0:T(8,128)(2,1)S(1)}, bf16[2,1024,128]{2,1,0:T(8,128)(2,1)S(1)}, f32[2,384,1024]{2,1,0:T(8,128)S(1)}, f32[2,384,1024]{2,1,...) custom-call(s32[1,12]{1,0:T(1,128)S(4)} %get-tuple-element.41.refs_0_, ...), custom_call_target="tpu_custom_call" | custom-call | flops 335544320 | bytes 2097152 | tf_op jit(solution)/shard_map/pallas_call | solution.py:334
  3.9 1.8 %collective-permute-start = (bf16[2,384,128]{2,1,0:T(8,128)(2,1)S(1)}, bf16[2,384,128]{2,1,0:T(8,128)(2,1)S(1)}, u32[]{:S(2)}, u32[]{:S(2)}) collective-permute-start(bf16[2,384,128]{2,1,0:T(8,128)(2,1)S(1)} %get-tuple-element.63.refs_4_.refs_9_), channel_id=1, source_target_pairs={{0,4},{4,8},{8,12},{1,5},{5,9},{9,13},{2,6},{6,10},{10,14},{3,7},{... | collective-permute-start | bytes 589832 | tf_op jit(solution)/shard_map/ppermute | solution.py:21
  5.7 3.1 %collective-permute-start.1 = (bf16[2,128,128]{2,1,0:T(8,128)(2,1)S(1)}, bf16[2,128,128]{2,1,0:T(8,128)(2,1)S(1)}, u32[]{:S(2)}, u32[]{:S(2)}) collective-permute-start(bf16[2,128,128]{2,1,0:T(8,128)(2,1)S(1)} %get-tuple-element.68), channel_id=1, source_target_pairs={{0,8},{4,12},{1,9},{5,13},{2,10},{6,14},{3,11},{7,15},{16,24},{20,... | collective-permute-start | bytes 196616 | tf_op jit(solution)/shard_map/ppermute | solution.py:21
  8.8 0.3 %shard_map.87 = (bf16[2,1024,128]{2,1,0:T(8,128)(2,1)S(1)}, bf16[2,1024,128]{2,1,0:T(8,128)(2,1)S(1)}, f32[2,384,1024]{2,1,0:T(8,128)S(1)}, f32[2,384,1024]{2,1,...) custom-call(s32[1,12]{1,0:T(1,128)S(4)} %get-tuple-element.41.refs_0, ...), custom_call_target="tpu_custom_call", output_to_operand_aliasing={{0}: (5, {}), {1}: (6, {}), {2}: (7, {}), {3}: (8, {}), {4}... | custom-call | flops 335544320 | bytes 2097152 | tf_op jit(solution)/shard_map/pallas_call | solution.py:334
  9.1 0.0 collective-permute-done.refs_4_.refs_10_
  9.1 0.1 shard_map.88
  9.2 1.7 %collective-permute-done.1.refs_10_.refs_11_ = bf16[2,128,128]{2,1,0:T(8,128)(2,1)S(1)} collective-permute-done((bf16[2,128,128]{2,1,0:T(8,128)(2,1)S(1)}, bf16[2,128,128]{2,1,0:T(8,128)(2,1)S(1)}, u32[]{:S(2)}, u32[]{:S(2)}) %collective-permute-start.1) | collective-permute-done | bytes 65568 | tf_op jit(solution)/shard_map/ppermute | solution.py:21
  10.8 0.2 shard_map.89
  11.0 1.3 %collective-permute-start.2 = (bf16[2,384,128]{2,1,0:T(8,128)(2,1)S(1)}, bf16[2,384,128]{2,1,0:T(8,128)(2,1)S(1)}, u32[]{:S(2)}, u32[]{:S(2)}) collective-permute-start(bf16[2,384,128]{2,1,0:T(8,128)(2,1)S(1)} %get-tuple-element.75), channel_id=1, source_target_pairs={{4,0},{8,4},{12,8},{5,1},{9,5},{13,9},{6,2},{10,6},{14,10},{7,3},{... | collective-permute-start | bytes 589832 | tf_op jit(solution)/shard_map/ppermute | solution.py:21
  12.3 1.3 %collective-permute-start.3 = (bf16[2,128,128]{2,1,0:T(8,128)(2,1)S(1)}, bf16[2,128,128]{2,1,0:T(8,128)(2,1)S(1)}, u32[]{:S(2)}, u32[]{:S(2)}) collective-permute-start(bf16[2,128,128]{2,1,0:T(8,128)(2,1)S(1)} %get-tuple-element.76), channel_id=1, source_target_pairs={{8,0},{12,4},{9,1},{13,5},{10,2},{14,6},{11,3},{15,7},{24,16},{28,... | collective-permute-start | bytes 196616 | tf_op jit(solution)/shard_map/ppermute | solution.py:21
  13.6 2.5 %shard_map.90 = (bf16[1,384,1024]{2,1,0:T(8,128)(2,1)}, f32[384,128]{1,0:T(8,128)S(1)}, f32[384,128]{1,0:T(8,128)S(1)}) custom-call(s32[1,12]{1,0:T(1,128)S(4)} %get-tuple-element.41.refs_0_, s32[1,12]{1,0:T(1,128)S(4)} %get-tuple-element.42.refs_1_, bf16[2,1024,128]{2,1,0:T(8,128)(2,1)S(1)} %get-tuple-element.57.refs_2_, ...), custom_call_target="tpu_custom_call" | custom-call | flops 838860800 | bytes 2097152 | tf_op jit(solution)/shard_map/pallas_call | solution.py:334
  16.2 4.2 %collective-permute-done.3.far_ref = bf16[2,128,128]{2,1,0:T(8,128)(2,1)S(1)} collective-permute-done((bf16[2,128,128]{2,1,0:T(8,128)(2,1)S(1)}, bf16[2,128,128]{2,1,0:T(8,128)(2,1)S(1)}, u32[]{:S(2)}, u32[]{:S(2)}) %collective-permute-start.3) | collective-permute-done | bytes 65568 | tf_op jit(solution)/shard_map/ppermute | solution.py:21
  20.4 0.0 collective-permute-done.2.near_ref
  20.4 0.7 %shard_map.91 = (bf16[1,384,128]{2,1,0:T(8,128)(2,1)}, bf16[1,384,128]{2,1,0:T(8,128)(2,1)}) custom-call(f32[384,128]{1,0:T(8,128)S(1)} %get-tuple-element.73.key_acc, f32[384,128]{1,0:T(8,128)S(1)} %get-tuple-element.74.value_acc, bf16[2,384,128]{2,1,0:T(8,128)(2,1)S(1)} %collective-permute-done.2.near_ref, ...), custom_call_target="tpu_custom_call" | custom-call | flops 256 | bytes 2097152 | tf_op jit(solution)/shard_map/pallas_call | solution.py:334
Async XLA Ops:
  3.9 5.2 %collective-permute-start = (bf16[2,384,128]{2,1,0:T(8,128)(2,1)S(1)}, bf16[2,384,128]{2,1,0:T(8,128)(2,1)S(1)}, u32[]{:S(2)}, u32[]{:S(2)}) collective-permute-start(bf16[2,384,128]{2,1,0:T(8,128)(2,1)S(1)} %get-tuple-element.63.refs_4_.refs_9_), channel_id=1, source_target_pairs={{0,4},{4,8},{8,12},{1,5},{5,9},{9,13},{2,6},{6,10},{10,14},{3,7},{... | collective-permute-start | bytes 589832 | tf_op jit(solution)/shard_map/ppermute | solution.py:21
  5.7 5.2 %collective-permute-start.1 = (bf16[2,128,128]{2,1,0:T(8,128)(2,1)S(1)}, bf16[2,128,128]{2,1,0:T(8,128)(2,1)S(1)}, u32[]{:S(2)}, u32[]{:S(2)}) collective-permute-start(bf16[2,128,128]{2,1,0:T(8,128)(2,1)S(1)} %get-tuple-element.68), channel_id=1, source_target_pairs={{0,8},{4,12},{1,9},{5,13},{2,10},{6,14},{3,11},{7,15},{16,24},{20,... | collective-permute-start | bytes 196616 | tf_op jit(solution)/shard_map/ppermute | solution.py:21
  11.0 9.4 %collective-permute-start.2 = (bf16[2,384,128]{2,1,0:T(8,128)(2,1)S(1)}, bf16[2,384,128]{2,1,0:T(8,128)(2,1)S(1)}, u32[]{:S(2)}, u32[]{:S(2)}) collective-permute-start(bf16[2,384,128]{2,1,0:T(8,128)(2,1)S(1)} %get-tuple-element.75), channel_id=1, source_target_pairs={{4,0},{8,4},{12,8},{5,1},{9,5},{13,9},{6,2},{10,6},{14,10},{7,3},{... | collective-permute-start | bytes 589832 | tf_op jit(solution)/shard_map/ppermute | solution.py:21
  12.3 8.1 %collective-permute-start.3 = (bf16[2,128,128]{2,1,0:T(8,128)(2,1)S(1)}, bf16[2,128,128]{2,1,0:T(8,128)(2,1)S(1)}, u32[]{:S(2)}, u32[]{:S(2)}) collective-permute-start(bf16[2,128,128]{2,1,0:T(8,128)(2,1)S(1)} %get-tuple-element.76), channel_id=1, source_target_pairs={{8,0},{12,4},{9,1},{13,5},{10,2},{14,6},{11,3},{15,7},{24,16},{28,... | collective-permute-start | bytes 196616 | tf_op jit(solution)/shard_map/ppermute | solution.py:21
